TPU v7x, 32 devices: a whole 2x2x4 slice. The times are simulated.
32 devices in a mesh: leaf: 4 (over y, core), front: 8 (over z, x).
Axes of the slice: x: 2, y: 2, z: 4, core: 2. Of those that a mesh axis runs over, the one named last changes fastest.
Arguments:
- child_fronts: float32 [4, 4096, 4, 8, 128], P('leaf', None, None, 'front'), as said below
- parent_front: float32 [16, 4, 128, 8, 8, 128], P(None, 'leaf', None, None, 'front'), as said below
- child_map: int32 [4, 24], replicated, may hold values from 0 to 63, as said below
Outputs:
- child_result: float32 [4, 4096, 4, 8, 128], P('leaf', None, None, 'front')
- parent_result: float32 [16, 4, 128, 8, 8, 128], P(None, 'leaf', None, None, 'front')
Inputs may be any that keep to these rules, and one draw needn't show every extreme that they name: Row g gives, for each update block v of child g, the parent block that receives it. The entries of a row are distinct, child_map[g, v] mod 8 equals (8 + v) mod 8, and every child's last update block goes to the parent's last block. `child_fronts`: each front is symmetric positive definite. `parent_front`: the parent front is symmetric positive definite.
All inputs are finite; a program needn't handle non-finite values.
Results may differ from a plain program's by a relative error of at most 0.000059.
Values sent between devices are 32-bit elements; how exact they have to be, the bound alone decides.
A program may use at most 256 MiB of HBM per device.

v0:
```python
import jax
import jax.numpy as jnp
from jax import lax
from jax.sharding import PartitionSpec as P

CHILD_PIVOTS = 8
PARENT_PIVOTS = 2


def from_root(value, axis, source):
    kept = jnp.where(lax.axis_index(axis) == source, value, 0).astype(value.dtype)
    return lax.psum(kept, axis)


def solve_rows(factor, rows):
    return jax.scipy.linalg.solve_triangular(factor, rows.T, lower=True).T


def body(child_fronts, parent_front, child_map):
    front_count = lax.axis_size("front")
    leaf_count = lax.axis_size("leaf")
    front_pos = lax.axis_index("front")
    leaf_pos = lax.axis_index("leaf")
    block = child_fronts.shape[4]
    child_order = child_fronts.shape[1]
    child_slots = child_fronts.shape[2]
    blocks_total = child_order // block
    pivots = CHILD_PIVOTS
    highest = lax.Precision.HIGHEST
    matrix = child_fronts.reshape(child_order, child_slots * block)
    column_ids = jnp.arange(child_slots * block) // block * front_count + front_pos
    slot_ids = jnp.arange(child_slots) * front_count + front_pos
    panel_slots = (pivots + front_count - 1) // front_count
    piece_rows = child_order // front_count
    width = pivots * block
    leading = matrix[:, : panel_slots * block].reshape(
        front_count, piece_rows, panel_slots, 1, block
    )
    spread = lax.all_to_all(leading, "front", split_axis=0, concat_axis=3, tiled=True)
    rows_part = spread.reshape(piece_rows, panel_slots * front_count * block)[:, :width]
    panel = lax.all_gather(rows_part, "front", axis=0, tiled=True)
    factored = []
    for pivot in range(pivots):
        start = pivot * block
        finish = start + block
        current = panel[:, start:finish]
        if factored:
            done = jnp.concatenate(factored, 1)
            current = current - jnp.dot(done, done[start:finish].T, precision=highest)
        factor = jnp.linalg.cholesky(current[start:finish])
        below = solve_rows(factor, current[finish:])
        factored.append(jnp.concatenate([jnp.zeros((start, block), jnp.float32), factor, below], 0))
    panel = jnp.concatenate(factored, 1)
    lower_rows = panel[width:]
    padded = jnp.concatenate([jnp.zeros((width, width), jnp.float32), lower_rows], 0)
    picked = jnp.take(padded.reshape(blocks_total, block, width), slot_ids, axis=0)
    picked = picked.reshape(child_slots * block, width)
    update = jnp.dot(lower_rows, picked.T, precision=highest)
    matrix = jnp.concatenate([matrix[:width], matrix[width:] - update], 0)
    pivot_columns = jnp.take(
        panel.reshape(child_order, pivots, block), jnp.clip(slot_ids, 0, pivots - 1), axis=1
    )
    pivot_columns = pivot_columns.reshape(child_order, child_slots * block)
    matrix = jnp.where((column_ids < pivots)[None, :], pivot_columns, matrix)
    row_blocks = jnp.arange(child_order) // block
    matrix = jnp.where(
        (row_blocks[:, None] < pivots) & (column_ids[None, :] >= pivots), 0.0, matrix
    )
    child_result = matrix.reshape(child_fronts.shape)
    first_slot = pivots // front_count
    update_count = blocks_total - pivots
    quota = update_count // leaf_count
    kept_slots = child_slots - first_slot
    outgoing = matrix[pivots * block :, first_slot * block :].reshape(
        quota, leaf_count, block, kept_slots, block
    )
    received = lax.all_to_all(outgoing, "leaf", split_axis=1, concat_axis=1, tiled=True)
    parent_rslots = parent_front.shape[0]
    parent_cslots = parent_front.shape[3]
    groups = child_map.shape[0]
    row_map = lax.dynamic_index_in_dim(
        child_map.reshape(groups, quota, leaf_count), leaf_pos, axis=2, keepdims=False
    )
    row_onehot = (
        (row_map // leaf_count)[:, :, None] == jnp.arange(parent_rslots)[None, None, :]
    ).astype(jnp.float32)
    col_blocks = jnp.arange(first_slot, child_slots) * front_count + front_pos - pivots
    valid = col_blocks >= 0
    col_map = jnp.take(child_map, jnp.clip(col_blocks, 0, update_count - 1), axis=1)
    col_match = (col_map // front_count)[:, :, None] == jnp.arange(parent_cslots)[None, None, :]
    col_onehot = (valid[None, :, None] & col_match).astype(jnp.float32)
    placed = jnp.einsum("gqa,qgxcy->gaxcy", row_onehot, received, precision=highest)
    summed = jnp.einsum("gcb,gaxcy->axby", col_onehot, placed, precision=highest)
    parent = parent_front.reshape(parent_rslots * block, parent_cslots * block)
    parent = parent + summed.reshape(parent_rslots * block, parent_cslots * block)
    prow_ids = jnp.arange(parent_rslots * block) // block * leaf_count + leaf_pos
    pcol_ids = jnp.arange(parent_cslots * block) // block * front_count + front_pos
    col_slot_ids = jnp.arange(parent_cslots) * front_count + front_pos
    parent_blocks = parent_rslots * leaf_count
    for pivot in range(PARENT_PIVOTS):
        col_root = pivot % front_count
        col_slot = pivot // front_count
        column = from_root(parent[:, col_slot * block : (col_slot + 1) * block], "front", col_root)
        whole = lax.all_gather(
            column.reshape(parent_rslots, 1, block, block), "leaf", axis=1, tiled=True
        )
        whole = whole.reshape(parent_blocks * block, block)
        factor = jnp.linalg.cholesky(whole[pivot * block : (pivot + 1) * block])
        above = jnp.arange(parent_blocks * block) // block <= pivot
        panel_all = jnp.where(above[:, None], 0.0, solve_rows(factor, whole))
        panel_local = lax.dynamic_index_in_dim(
            panel_all.reshape(parent_rslots, leaf_count, block, block),
            leaf_pos,
            axis=1,
            keepdims=False,
        )
        panel_local = panel_local.reshape(parent_rslots * block, block)
        panel_cols = jnp.take(panel_all.reshape(parent_blocks, block, block), col_slot_ids, axis=0)
        panel_cols = panel_cols.reshape(parent_cslots * block, block)
        parent = parent - jnp.dot(panel_local, panel_cols.T, precision=highest)
        new_column = jnp.where(
            (prow_ids == pivot)[:, None], jnp.tile(factor, (parent_rslots, 1)), panel_local
        )
        parent = jnp.where(
            (pcol_ids == pivot)[None, :], jnp.tile(new_column, (1, parent_cslots)), parent
        )
    parent = jnp.where(
        (prow_ids[:, None] < PARENT_PIVOTS) & (pcol_ids[None, :] >= PARENT_PIVOTS), 0.0, parent
    )
    parent_result = parent.reshape(parent_front.shape)
    return (child_result, parent_result)


def solution(mesh):
    return jax.shard_map(
        body,
        mesh=mesh,
        in_specs=(
            P("leaf", None, None, "front", None),
            P(None, "leaf", None, None, "front", None),
            P(),
        ),
        out_specs=(
            P("leaf", None, None, "front", None),
            P(None, "leaf", None, None, "front", None),
        ),
        check_vma=False,
    )
```

profile of v0, /device:TPU:0, one launch (start us, length us, event | category | flops | bytes accessed | tf_op | source)
XLA Modules:
  0.0 1231.8 jit_solution(14088938712485502116)
XLA Ops:
  11.9 55.3 %all_to_all.20 = f32[8,512,1,1,128]{4,1,3,2,0:T(8,128)S(1)} all-to-all(f32[8,512,1,1,128]{4,1,3,2,0:T(8,128)S(1)} %bitcast.247), channel_id=1, replica_groups=mesh['leaf'=4,'front'=8] {'front'}, dimensions={0} | all-to-all | bytes 4194304 | tf_op jit(solution)/shard_map/all_to_all | solution.py:39
  79.3 14.3 %copy.185 = f32[1,3072,4,1,128]{1,4,2,3,0:T(8,128)} copy(f32[1,3072,4,1,128]{4,3,2,1,0:T(1,128)} %slice.214) | data formatting | bytes 12582912 | tf_op jit(solution)/shard_map/slice | solution.py:59
  98.5 197.2 %all-gather.4.cloned.1.call-done = f32[4096,1024]{0,1:T(8,128)} async-done(((f32[512,1024]{0,1:T(8,128)}), f32[4096,1024]{0,1:T(8,128)}) %all-gather.4.cloned.1.call-update) | async-done | bytes 16777232 | tf_op jit(solution)/shard_map/all_gather | solution.py:41
  297.6 11.7 cholesky.164
  334.2 11.9 cholesky.175
  369.2 12.1 cholesky.186
  407.1 11.7 cholesky.197
  447.3 11.7 cholesky.208
  501.9 11.7 cholesky.219
  543.3 11.7 cholesky.230
  573.0 12.8 %convolution_subtract_fusion.4 = f32[4096,128]{0,1:T(8,128)S(1)} fusion(f32[4096,896]{0,1:T(8,128)} %get-tuple-element.56, f32[4096,1024]{0,1:T(8,128)} %all-gather.4.cloned.1.call-done), kind=kOutput, calls=%fused_computation.66 | convolution fusion | flops 5637668864 | bytes 19333120 | tf_op jit(solution)/shard_map/dot_general | solution.py:49
  585.9 11.7 cholesky.241
  625.2 12.6 %copy.238 = f32[3072,1024]{1,0:T(8,128)} copy(f32[3072,1024]{0,1:T(8,128)} %slice.261) | data formatting | bytes 25165824
  637.8 11.8 concatenate.77.clone
  649.6 17.4 %copy.183 = f32[4096,8,128]{2,0,1:T(8,128)} copy(f32[4096,8,128]{0,2,1:T(8,128)} %bitcast.229) | data formatting | bytes 33554432 | tf_op jit(solution)/shard_map/reshape | solution.py:61
  692.9 24.6 %bitcast_subtract_fusion = f32[3072,512]{0,1:T(8,128)S(1)} fusion(f32[1,3072,4,1,128]{1,4,2,3,0:T(8,128)} %copy.185, f32[512,1024]{1,0:T(8,128)S(1)} %bitcast_select_fusion.3, f32[4096,1024]{0,1:T(8,128)} %maximum_dynamic-update-slice_fusion), kind=kOutput, calls=%fused_computation.58 | convolution fusion | flops 19328925696 | bytes 27262976 | tf_op jit(solution)/shard_map/dot_general | solution.py:58
  742.5 52.7 %all-to-all-done.1 = f32[6,4,128,3,128]{4,2,3,0,1:T(8,128)} async-done(((f32[6,4,128,3,128]{4,2,3,0,1:T(8,128)}), f32[6,4,128,3,128]{4,2,3,0,1:T(8,128)}, u32[]{:S(2)}, u32[]{:S(2)}) %all-to-all-start.1) | async-done | bytes 4718624 | tf_op jit(solution)/shard_map/all_to_all | solution.py:77
  806.1 16.0 %fusion = f32[16,128,128,8,1]{2,3,4,1,0:T(8,128)} fusion(f32[4,16,128,3,128]{4,1,3,2,0:T(8,128)S(1)} %fusion.45, s32[4,3]{0,1:T(4,128)S(1)} %add_select_fusion.5, pred[3]{0:T(512)(128)(4,1)S(1)} %get-tuple-element.61), kind=kOutput, calls=%fused_computation.5 | convolution fusion | flops 301990080 | bytes 20971572 | tf_op jit(solution)/shard_map/gcb,gaxcy->axby/dot_general | solution.py:93
  822.1 13.2 %bitcast_add_fusion = f32[2048,1024]{1,0:T(8,128)} fusion(f32[256,8,8,128]{3,2,1,0:T(8,128)} %bitcast.232, f32[256,8,8,128]{3,2,1,0:T(8,128)} %bitcast.243), kind=kLoop, calls=%fused_computation.15 | loop fusion | flops 2097152 | bytes 25165824 | tf_op jit(solution)/shard_map/add | solution.py:95
  837.6 75.5 %all-reduce.4.cloned.1.call-done = f32[16,1,128,128]{3,2,0,1:T(8,128)} async-done(((f32[16,1,128,128]{3,2,0,1:T(8,128)}), f32[16,1,128,128]{3,2,0,1:T(8,128)}) %all-reduce.4.cloned.1.call-update) | async-done | bytes 1048592 | tf_op jit(solution)/shard_map/psum | solution.py:12
  913.3 35.6 %all-gather.6.cloned.1.call-done = f32[16,4,128,128]{3,2,0,1:T(8,128)} async-done(((f32[16,1,128,128]{3,2,0,1:T(8,128)}), f32[16,4,128,128]{3,2,0,1:T(8,128)}) %all-gather.6.cloned.1.call-update) | async-done | bytes 4194320 | tf_op jit(solution)/shard_map/all_gather | solution.py:104
  962.2 11.7 cholesky.252
  1028.0 78.2 %all-reduce.6.cloned.1.call-done = f32[16,1,128,128]{3,2,0,1:T(8,128)} async-done(((f32[16,1,128,128]{3,2,0,1:T(8,128)}), f32[16,1,128,128]{3,2,0,1:T(8,128)}) %all-reduce.6.cloned.1.call-update) | async-done | bytes 1048592 | tf_op jit(solution)/shard_map/psum | solution.py:12
  1122.0 22.8 %copy.202 = f32[1,4096,4,1,128]{4,3,2,1,0:T(1,128)} copy(f32[1,4096,4,1,128]{4,1,2,3,0:T(8,128)S(1)} %fusion.28) | data formatting | bytes 16777216
  (243 shorter events, 470.8 us)
Async XLA Ops:
  7.2 288.6 %all-gather.4.cloned.1.call-start = ((), (), s32[]{:S(2)}) async-start(), calls=%async_computation.2 | async-start | bytes 18874368 | tf_op jit(solution)/shard_map/all_gather | solution.py:41
  79.2 14.6 %copy-start.3 = (f32[1,1024,4,1,128]{4,3,2,1,0:T(1,128)}, f32[1,1024,4,1,128]{4,3,2,1,0:T(1,128)S(1)}, u32[]{:S(2)}) copy-start(f32[1,1024,4,1,128]{4,3,2,1,0:T(1,128)S(1)} %slice.213) | copy-start | bytes 6291460
  93.6 217.0 %copy-start.17 = (pred[4]{0:T(512)(128)(4,1)}, pred[4]{0:T(512)(128)(4,1)S(1)}, u32[]{:S(2)}) copy-start(pred[4]{0:T(512)(128)(4,1)S(1)} %get-tuple-element.63) | copy-start | bytes 16
  98.4 229.8 %copy-start.14 = (pred[4096]{0:T(1024)(128)(4,1)}, pred[4096]{0:T(1024)(128)(4,1)S(1)}, u32[]{:S(2)}) copy-start(pred[4096]{0:T(1024)(128)(4,1)S(1)} %fusion.196) | copy-start | bytes 12292
  446.2 28.3 %copy-start.2 = (f32[3840,128]{0,1:T(8,128)S(1)}, f32[3840,128]{0,1:T(8,128)}, u32[]{:S(2)}) copy-start(f32[3840,128]{0,1:T(8,128)} %fusion.67) | copy-start | bytes 5898244
  474.5 4.4 copy-start.9
  478.9 4.3 copy-start.10
  483.3 4.2 copy-start.11
  692.6 27.6 %slice-start = ((s8[8388608]{0:T(1024)(128)(4,1)}), s8[4194304]{0:T(1024)(128)(4,1)S(1)}, s32[]{:S(2)}) async-start(s8[8388608]{0:T(1024)(128)(4,1)} %bitcast.237), calls=%async_computation.7 | async-start | bytes 8388608
  692.8 27.3 %slice-start.1 = ((s8[8388608]{0:T(1024)(128)(4,1)}), s8[4194304]{0:T(1024)(128)(4,1)S(1)}, s32[]{:S(2)}) async-start(s8[8388608]{0:T(1024)(128)(4,1)} %bitcast.237), calls=%async_computation.8 | async-start | bytes 8388608
  692.8 27.3 %copy-start.5 = (f32[1,1024,4,1,128]{1,4,2,3,0:T(8,128)S(1)}, f32[1,1024,4,1,128]{1,4,2,3,0:T(8,128)}, u32[]{:S(2)}) copy-start(f32[1,1024,4,1,128]{1,4,2,3,0:T(8,128)} %copy.189) | copy-start | bytes 6291460
  692.8 27.3 %slice-start.2 = ((pred[4096]{0:T(1024)(128)(4,1)}), pred[3072]{0:T(1024)(128)(4,1)S(1)}, s32[]{:S(2)}) async-start(pred[4096]{0:T(1024)(128)(4,1)} %copy-done.14), calls=%async_computation.9 | async-start | bytes 6144 | tf_op jit(solution)/shard_map/slice | solution.py:74
  717.4 2.7 copy-start
  736.3 5.1 copy-start.16
  736.3 58.9 %all-to-all-start.1 = ((f32[6,4,128,3,128]{4,2,3,0,1:T(8,128)}), f32[6,4,128,3,128]{4,2,3,0,1:T(8,128)}, u32[]{:S(2)}, u32[]{:S(2)}) async-start(f32[6,4,128,3,128]{4,2,3,0,1:T(8,128)} %copy.190), calls=%async_computation.1 | async-start | bytes 9437184 | tf_op jit(solution)/shard_map/all_to_all | solution.py:77
  741.3 171.8 %all-reduce.4.cloned.1.call-start = ((), (), s32[]{:S(2)}) async-start(), calls=%async_computation.3 | async-start | bytes 2097152 | tf_op jit(solution)/shard_map/psum | solution.py:12
  837.6 111.3 %all-gather.6.cloned.1.call-start = ((), (), s32[]{:S(2)}) async-start(), calls=%async_computation.4 | async-start | bytes 5242880 | tf_op jit(solution)/shard_map/all_gather | solution.py:104
  913.2 193.0 %all-reduce.6.cloned.1.call-start = ((), (), s32[]{:S(2)}) async-start(), calls=%async_computation.5 | async-start | bytes 2097152 | tf_op jit(solution)/shard_map/psum | solution.py:12
  1023.5 3.2 copy-start.1
  1026.8 79.5 %copy-start.4 = (f32[1,1024,4,1,128]{4,3,2,1,0:T(1,128)S(1)}, f32[1,1024,4,1,128]{4,3,2,1,0:T(1,128)}, u32[]{:S(2)}) copy-start(f32[1,1024,4,1,128]{4,3,2,1,0:T(1,128)} %copy-done.3) | copy-start | bytes 6291460
  1027.9 116.9 %all-gather.8.cloned.1.call-start = ((), (), s32[]{:S(2)}) async-start(), calls=%async_computation.6 | async-start | bytes 5242880 | tf_op jit(solution)/shard_map/all_gather | solution.py:104
  1107.7 6.7 copy-start.6
  1107.7 6.7 copy-start.15
  1107.7 6.7 copy-start.18
  (4 other events, 5.3 us)
Sparse Core Ops, SparseCore 0:
  69.1 226.6 all-gather.3
  837.7 75.4 all-reduce.3
  914.8 34.0 all-gather.5
  1028.0 78.1 all-reduce.5
  1107.6 34.0 all-gather.7
where the time goes:
time: 1240 us; the launch traced here: 1230 us
  waiting for transfers between devices  439 us (35%)
  other arithmetic  297 us (24%)
  local copies, waits for them, and re-layouts  241 us (19%)
  matrix products  179 us (14%)
  blocking collectives  55.3 us (4%)
  between operations  15.1 us (1%)
    all_gather x1, waiting for transfers between devices, body(): panel = lax.all_gather(rows_part, 'front', axis=0, tiled=True)  197 us
    psum x2, waiting for transfers between devices, from_root(): return lax.psum(kept, axis)  154 us
    another operation x20, other arithmetic, solve_rows(): return jax.scipy.linalg.solve_triangular(factor, rows.T, lower=True).T  105 us
    another operation x24, other arithmetic, body(): factor = jnp.linalg.cholesky(current[start:finish])  99.8 us
    dot_general x7, matrix products, body(): current = current - jnp.dot(done, done[start:finish].T, precision=highest)  59.7 us
    unnamed x50, local copies, waits for them, and re-layouts  59.4 us
    all_to_all x1, blocking collectives, body(): lax.all_to_all(leading, 'front', split_axis=0, concat_axis=3, tiled=True)  55.3 us
    all_to_all x1, waiting for transfers between devices, body(): lax.all_to_all(outgoing, 'leaf', split_axis=1, concat_axis=1, tiled=True)  52.7 us
  transfers between devices with their start and end apart: 6, of which 5 were waited for; matrix products, arithmetic and copies ran while one was open for 6% of the time, Pallas kernels for 0%

commit v1 on v0

v1 whole, which is shorter than its diff:
```python
import jax
import jax.numpy as jnp
from jax import lax
from jax.sharding import PartitionSpec as P

CHILD_PIVOTS = 8
PARENT_PIVOTS = 2
HIGH = lax.Precision.HIGH
HIGHEST = lax.Precision.HIGHEST


def factor_block(square):
    return lax.linalg.cholesky(square, symmetrize_input=False)


def solve_left(factor, rows):
    return lax.linalg.triangular_solve(factor, rows, left_side=True, lower=True)


def factor_strips(work, pivots, block):
    strips = []
    for i in range(pivots):
        start = i * block
        current = work[start : start + block, start:]
        if strips:
            done = jnp.concatenate(
                [strip[:, (i - j) * block :] for j, strip in enumerate(strips)], 0
            )
            current = current - lax.dot_general(
                done[:, :block], done, (((0,), (0,)), ((), ())), precision=HIGHEST
            )
        factor = factor_block(current[:, :block])
        rest = solve_left(factor, current[:, block:])
        strips.append(jnp.concatenate([factor.T, rest], 1))
    return strips


def body(child_fronts, parent_front, child_map):
    front_count = lax.axis_size("front")
    leaf_count = lax.axis_size("leaf")
    front_pos = lax.axis_index("front")
    leaf_pos = lax.axis_index("leaf")
    block = child_fronts.shape[4]
    order = child_fronts.shape[1]
    slots = child_fronts.shape[2]
    pivots = CHILD_PIVOTS
    width = pivots * block
    first_slot = pivots // front_count
    kept = slots - first_slot
    panel_slots = (pivots + front_count - 1) // front_count
    update_count = order // block - pivots
    matrix = child_fronts.reshape(order, slots * block)

    lead = lax.all_gather(matrix[:width, : panel_slots * block], "front", axis=0)
    lead = lead.reshape(front_count, width, panel_slots, block).transpose(1, 2, 0, 3)
    lead = lead.reshape(width, panel_slots * front_count * block)[:, :width]

    own_top = matrix[:width, first_slot * block :]
    strips = factor_strips(jnp.concatenate([lead, own_top], 1), pivots, block)
    gathered = []
    own = []
    lead_columns = []
    for i, strip in enumerate(strips):
        split = width - i * block
        own.append(strip[:, split:])
        gathered.append(
            lax.all_gather(strip[:, split:].T, "front", axis=0, tiled=True).reshape(
                front_count, kept, block, block
            )
        )
        column = strip[:, :split].T
        lead_columns.append(
            jnp.concatenate([jnp.zeros((i * block, block), jnp.float32), column], 0)
        )
    own = jnp.concatenate(own, 0)
    lower = jnp.concatenate(gathered, 3).transpose(1, 0, 2, 3)
    lower = lower.reshape(kept * front_count * block, width)
    lower = lower[width - first_slot * front_count * block :]

    parts = kept if update_count % (kept * leaf_count) == 0 else 1
    part_rows = update_count * block // parts
    sums = []
    received = []
    for part in range(parts):
        low = part * part_rows
        product = lax.dot_general(
            lower[low : low + part_rows], own, (((1,), (0,)), ((), ())), precision=HIGH
        )
        piece = matrix[width + low : width + low + part_rows, first_slot * block :] - product
        sums.append(piece)
        outgoing = piece.reshape(
            part_rows // block // leaf_count, leaf_count, block, kept, block
        )
        received.append(
            lax.all_to_all(outgoing, "leaf", split_axis=1, concat_axis=1, tiled=True)
        )
    received = jnp.concatenate(received, 0)
    update = jnp.concatenate(sums, 0)

    all_leads = jnp.concatenate(lead_columns, 1)
    columns = []
    for slot in range(slots):
        pick = jnp.clip(slot * front_count + front_pos, 0, pivots - 1) * block
        if slot < panel_slots:
            pivot_column = jnp.concatenate(
                [
                    lax.dynamic_slice_in_dim(all_leads, pick, block, 1),
                    lax.dynamic_slice_in_dim(lower, pick, block, 1),
                ],
                0,
            )
        if slot < first_slot:
            columns.append(pivot_column)
            continue
        at = (slot - first_slot) * block
        column = jnp.concatenate(
            [jnp.zeros((width, block), jnp.float32), update[:, at : at + block]], 0
        )
        if slot < panel_slots:
            is_pivot = slot * front_count + front_pos < pivots
            column = jnp.where(is_pivot, pivot_column, column)
        columns.append(column)
    child_result = jnp.stack(columns, 1).reshape(child_fronts.shape)

    rslots = parent_front.shape[0]
    cslots = parent_front.shape[3]
    groups = child_map.shape[0]
    quota = update_count // leaf_count
    row_map = lax.dynamic_index_in_dim(
        child_map.reshape(groups, quota, leaf_count), leaf_pos, axis=2, keepdims=False
    )
    row_onehot = (
        (row_map // leaf_count)[:, :, None] == jnp.arange(rslots)[None, None, :]
    ).astype(jnp.float32)
    col_blocks = jnp.arange(first_slot, slots) * front_count + front_pos - pivots
    valid = col_blocks >= 0
    col_map = jnp.take(child_map, jnp.clip(col_blocks, 0, update_count - 1), axis=1)
    col_match = (col_map // front_count)[:, :, None] == jnp.arange(cslots)[None, None, :]
    col_onehot = (valid[None, :, None] & col_match).astype(jnp.float32)
    placed = jnp.einsum("gqa,qgxcy->gaxcy", row_onehot, received, precision=HIGH)
    summed = jnp.einsum("gcb,gaxcy->axby", col_onehot, placed, precision=HIGH)
    parent = parent_front.reshape(rslots * block, cslots * block)
    parent = parent + summed.reshape(rslots * block, cslots * block)

    count = PARENT_PIVOTS
    span = count * block
    row_panel = lax.all_gather(parent[:block], "leaf", axis=0)[:count]
    row_panel = row_panel.reshape(span, cslots * block)
    spread = lax.all_to_all(
        parent[:, :block].reshape(front_count, rslots * block // front_count, block),
        "front",
        split_axis=0,
        concat_axis=0,
        tiled=True,
    )[:count]
    spread = spread.transpose(1, 0, 2).reshape(rslots * block // front_count, span)
    col_panel = lax.all_gather(spread, "front", axis=0, tiled=True)
    square = lax.all_gather(col_panel[:block], "leaf", axis=0)[:count].reshape(span, span)
    work = jnp.concatenate([square, row_panel, col_panel.T], 1)
    strips = factor_strips(work, count, block)
    row_done = jnp.concatenate(
        [strip[:, (count - i) * block : (count - i + cslots) * block] for i, strip in enumerate(strips)], 0
    )
    col_done = jnp.concatenate(
        [strip[:, (count - i + cslots) * block :] for i, strip in enumerate(strips)], 0
    )
    factor = jnp.concatenate(
        [
            jnp.concatenate(
                [jnp.zeros((i * block, block), jnp.float32), strip[:, : span - i * block].T], 0
            )
            for i, strip in enumerate(strips)
        ],
        1,
    )
    columns_done = col_done.T
    product = lax.dot_general(
        columns_done, row_done, (((1,), (0,)), ((), ())), precision=HIGH
    )
    trailing = parent - product
    mine = jnp.clip(front_pos, 0, count - 1) * block
    pivot_column = lax.dynamic_slice_in_dim(columns_done, mine, block, 1)
    row_pick = jnp.clip(leaf_pos, 0, count - 1) * block
    head = lax.dynamic_slice(factor, (row_pick, mine), (block, block))
    row_is_pivot = leaf_pos < count
    col_is_pivot = front_pos < count
    pivot_column = jnp.concatenate(
        [jnp.where(row_is_pivot, head, pivot_column[:block]), pivot_column[block:]], 0
    )
    row_ids = jnp.arange(rslots * block)[:, None] < block
    trailing = jnp.where(row_is_pivot & row_ids, 0.0, trailing)
    first = jnp.where(col_is_pivot, pivot_column, trailing[:, :block])
    parent_result = jnp.concatenate([first, trailing[:, block:]], 1)
    return (child_result, parent_result.reshape(parent_front.shape))


def solution(mesh):
    return jax.shard_map(
        body,
        mesh=mesh,
        in_specs=(
            P("leaf", None, None, "front", None),
            P(None, "leaf", None, None, "front", None),
            P(),
        ),
        out_specs=(
            P("leaf", None, None, "front", None),
            P(None, "leaf", None, None, "front", None),
        ),
        check_vma=False,
    )
```

time: 1240 us -> 820 us (0.66)
  waiting for transfers between devices: 439 us -> 231 us
  matrix products: 179 us -> 93.4 us
  local copies, waits for them, and re-layouts: 241 us -> 186 us
  blocking collectives: 55.3 us -> 7.36 us
  other arithmetic: 297 us -> 257 us
  starting transfers between devices: 5.27 us -> 19 us
    psum x2 -> x0, waiting for transfers between devices: 154 us -> none  [from_root(): return lax.psum(kept, axis)]
    dot_general x12 -> x14, matrix products: 133 us -> 76.7 us  [the longest x1 22.1 us: body(): summed = jnp.einsum('gcb,gaxcy->axby', col_onehot, placed, precision=HIGH)]
    all_to_all x1 -> x0, blocking collectives: 55.3 us -> none  [body(): lax.all_to_all(leading, 'front', split_axis=0, concat_axis=3, tiled=True)]
    reshape x9 -> x6, local copies, waits for them, and re-layouts: 65.5 us -> 19.3 us  [body(): piece.reshape(part_rows // block // leaf_count, leaf_count, block, kept,...]
    all_gather x3 -> x11, waiting for transfers between devices: 233 us -> 193 us  [the longest x8 111 us: body(): lax.all_gather(strip[:, split:].T, 'front', axis=0, tiled=True)]
    gather x5 -> x0, local copies, waits for them, and re-layouts: 31.2 us -> none  [the longest x2 19.2 us: body(): jnp.take(panel.reshape(child_order, pivots, block), jnp.clip(slot_ids, 0,...]
    another operation x10, matrix products: 45.8 us -> 16.7 us  [solve_left(): return lax.linalg.triangular_solve(factor, rows, left_side=True, lower=True)]
    all_to_all x1 -> x3, waiting for transfers between devices: 52.7 us -> 24.7 us  [body(): lax.all_to_all(outgoing, 'leaf', split_axis=1, concat_axis=1, tiled=True)]
  transfers between devices with their start and end apart: 6 -> 15, of which waited for: 5 -> 9; matrix products, arithmetic and copies ran while one was open for 6% -> 41% of each run, Pallas kernels for 0% -> 0%
where the time goes in v1:
time: 820 us; the launch traced here: 809 us
  other arithmetic  257 us (31%)
  waiting for transfers between devices  231 us (28%)
  local copies, waits for them, and re-layouts  186 us (23%)
  matrix products  93.4 us (11%)
  starting transfers between devices  19 us (2%)
  between operations  15.5 us (2%)
    another operation x30, other arithmetic, factor_block(): return lax.linalg.cholesky(square, symmetrize_input=False)  124 us
    all_gather x8, waiting for transfers between devices, body(): lax.all_gather(strip[:, split:].T, 'front', axis=0, tiled=True)  111 us
    another operation x12, other arithmetic, solve_left(): return lax.linalg.triangular_solve(factor, rows, left_side=True, lower=True)  101 us
    unnamed x145, local copies, waits for them, and re-layouts  81.1 us
    all_gather x1, waiting for transfers between devices, body(): lead = lax.all_gather(matrix[:width, :panel_slots * block], 'front', axis=0)  74.7 us
    all_to_all x3, waiting for transfers between devices, body(): lax.all_to_all(outgoing, 'leaf', split_axis=1, concat_axis=1, tiled=True)  24.7 us
    dot_general x1, matrix products, body(): summed = jnp.einsum('gcb,gaxcy->axby', col_onehot, placed, precision=HIGH)  22.1 us
    all_gather x8, local copies, waits for them, and re-layouts, body(): lax.all_gather(strip[:, split:].T, 'front', axis=0, tiled=True)  22.1 us
  transfers between devices with their start and end apart: 15, of which 9 were waited for; matrix products, arithmetic and copies ran while one was open for 41% of the time, Pallas kernels for 0%

profile of v1, /device:TPU:0, one launch (start us, length us, event | category | flops | bytes accessed | tf_op | source)
XLA Modules:
  0.0 809.2 jit_solution(12851219259545103661)
XLA Ops:
  17.4 74.7 %all-gather.33.cloned.1.call-done = f32[8192,128]{1,0:T(8,128)} async-done(((f32[1024,128]{1,0:T(8,128)}), f32[8192,128]{1,0:T(8,128)}) %all-gather.33.cloned.1.call-update) | async-done | bytes 4194320 | tf_op jit(solution)/shard_map/all_gather | solution.py:54
  99.8 11.7 %custom-call.52 = f32[128,128]{1,0:T(8,128)S(1)} custom-call(f32[128,128]{1,0:T(8,128)S(1)} %slice.443), custom_call_target="Cholesky" | custom-call | tf_op jit(solution)/shard_map/cholesky/custom-call.1 | solution.py:13
  128.9 11.7 %custom-call.53 = f32[128,128]{1,0:T(8,128)S(1)} custom-call(f32[128,128]{1,0:T(8,128)S(1)} %slice.446), custom_call_target="Cholesky" | custom-call | tf_op jit(solution)/shard_map/cholesky/custom-call.1 | solution.py:13
  157.9 11.7 %custom-call.54 = f32[128,128]{1,0:T(8,128)S(1)} custom-call(f32[128,128]{1,0:T(8,128)S(1)} %slice.448), custom_call_target="Cholesky" | custom-call | tf_op jit(solution)/shard_map/cholesky/custom-call.1 | solution.py:13
  171.7 9.8 %custom-call.35 = f32[1,128,128]{1,2,0:T(8,128)S(1)} custom-call(f32[1,128,128]{2,1,0:T(8,128)S(1)} %get-tuple-element.44), custom_call_target="InvertDiagBlocksLowerTriangular" | custom-call | tf_op jit(solution)/shard_map/triangular_solve | solution.py:17
  189.3 11.7 %custom-call.55 = f32[128,128]{1,0:T(8,128)S(1)} custom-call(f32[128,128]{1,0:T(8,128)S(1)} %slice.451), custom_call_target="Cholesky" | custom-call | tf_op jit(solution)/shard_map/cholesky/custom-call.1 | solution.py:13
  203.0 9.8 %custom-call.36 = f32[1,128,128]{1,2,0:T(8,128)S(1)} custom-call(f32[1,128,128]{2,1,0:T(8,128)S(1)} %get-tuple-element.42), custom_call_target="InvertDiagBlocksLowerTriangular" | custom-call | tf_op jit(solution)/shard_map/triangular_solve | solution.py:17
  219.9 11.7 %custom-call.56 = f32[128,128]{1,0:T(8,128)S(1)} custom-call(f32[128,128]{1,0:T(8,128)S(1)} %slice.455), custom_call_target="Cholesky" | custom-call | tf_op jit(solution)/shard_map/cholesky/custom-call.1 | solution.py:13
  250.9 11.7 %custom-call.57 = f32[128,128]{1,0:T(8,128)S(1)} custom-call(f32[128,128]{1,0:T(8,128)S(1)} %slice.461), custom_call_target="Cholesky" | custom-call | tf_op jit(solution)/shard_map/cholesky/custom-call.1 | solution.py:13
  281.6 11.7 %custom-call.58 = f32[128,128]{1,0:T(8,128)S(1)} custom-call(f32[128,128]{1,0:T(8,128)S(1)} %slice.468), custom_call_target="Cholesky" | custom-call | tf_op jit(solution)/shard_map/cholesky/custom-call.1 | solution.py:13
  295.2 10.4 %custom-call.39 = f32[1,128,128]{1,2,0:T(8,128)} custom-call(f32[1,128,128]{2,1,0:T(8,128)S(1)} %get-tuple-element.36), custom_call_target="InvertDiagBlocksLowerTriangular" | custom-call | tf_op jit(solution)/shard_map/triangular_solve | solution.py:17
  317.2 11.7 %custom-call.59 = f32[128,128]{1,0:T(8,128)S(1)} custom-call(f32[128,128]{1,0:T(8,128)S(1)} %slice.476), custom_call_target="Cholesky" | custom-call | tf_op jit(solution)/shard_map/cholesky/custom-call.1 | solution.py:13
  356.9 38.6 %all-gather.25.cloned.1.call-done = f32[3072,128]{0,1:T(8,128)} async-done(((f32[384,128]{0,1:T(8,128)}), f32[3072,128]{0,1:T(8,128)}) %all-gather.25.cloned.1.call-update) | async-done | bytes 1572880 | tf_op jit(solution)/shard_map/all_gather | solution.py:67
  398.6 42.0 %all-gather.27.cloned.1.call-done = f32[3072,128]{0,1:T(8,128)} async-done(((f32[384,128]{0,1:T(8,128)}), f32[3072,128]{0,1:T(8,128)}) %all-gather.27.cloned.1.call-update) | async-done | bytes 1572880 | tf_op jit(solution)/shard_map/all_gather | solution.py:67
  455.1 30.7 %all-gather.29.cloned.1.call-done = f32[3072,128]{0,1:T(8,128)} async-done(((f32[384,128]{0,1:T(8,128)}), f32[3072,128]{0,1:T(8,128)}) %all-gather.29.cloned.1.call-update) | async-done | bytes 1572880 | tf_op jit(solution)/shard_map/all_gather | solution.py:67
  489.0 10.5 %fusion.135 = (f32[1,8,128,1024]{3,2,0,1:T(8,128)}, f32[1,8,128,1024]{3,2,0,1:T(8,128)}, f32[1,8,128,1024]{3,2,0,1:T(8,128)S(1)}) fusion(f32[3,8,128,1024]{3,2,0,1:T(8,128)} %bitcast.48), kind=kLoop, calls=%fused_computation.281 | loop fusion | bytes 25165824 | tf_op jit(solution)/shard_map/slice | solution.py:87
  588.3 10.3 %fusion.2 = f32[4,16,128,3,128]{4,1,3,2,0:T(8,128)} fusion(f32[2,4,128,3,128]{4,0,3,2,1:T(2,128)} %copy.86, f32[2,4,128,3,128]{4,0,3,2,1:T(2,128)} %copy.85, f32[2,4,128,3,128]{4,0,3,2,1:T(2,128)} %copy.84, s32[4,6]{1,0:T(4,128)S(1)} %fusion.113), kind=kOutput, calls=%fused_computation.8 | convolution fusion | flops 115605888 | bytes 17301600 | tf_op jit(solution)/shard_map/gqa,qgxcy->gaxcy/dot_general | solution.py:140
  598.7 22.1 %fusion = f32[16,128,128,8,1]{2,3,4,1,0:T(8,128)} fusion(f32[4,16,128,3,128]{4,1,3,2,0:T(8,128)} %fusion.2, s32[4,3]{0,1:T(4,128)S(1)} %add_select_fusion.1, pred[3]{0:T(512)(128)(4,1)S(1)} %get-tuple-element.60), kind=kOutput, calls=%fused_computation.1 | convolution fusion | flops 150995136 | bytes 20971572 | tf_op jit(solution)/shard_map/gcb,gaxcy->axby/dot_general | solution.py:141
  620.7 13.4 %bitcast_add_fusion = f32[2048,1024]{1,0:T(8,128)} fusion(f32[256,8,8,128]{3,2,1,0:T(8,128)} %bitcast.221, f32[256,8,8,128]{3,2,1,0:T(8,128)} %bitcast.234), kind=kLoop, calls=%fused_computation.3 | loop fusion | flops 2097152 | bytes 25165824 | tf_op jit(solution)/shard_map/add | solution.py:143
  656.1 12.4 %all-to-all-done.3 = f32[8,256,128]{2,1,0:T(8,128)} async-done(((f32[8,256,128]{2,1,0:T(8,128)}), f32[8,256,128]{2,1,0:T(8,128)}, u32[]{:S(2)}, u32[]{:S(2)}) %all-to-all-start.3) | async-done | bytes 1048608 | tf_op jit(solution)/shard_map/all_to_all | solution.py:149
  672.3 12.2 %copy.77 = f32[3,8,128,1024]{3,2,1,0:T(8,128)} copy(f32[3,8,128,1024]{3,2,0,1:T(8,128)} %bitcast.48) | data formatting | bytes 25165824 | tf_op jit(solution)/shard_map/transpose | solution.py:76
  688.6 22.8 %copy.96 = f32[1,4096,4,1,128]{4,3,2,1,0:T(1,128)} copy(f32[1,4096,4,1,128]{4,1,2,3,0:T(8,128)S(1)} %maximum_bitcast_fusion) | data formatting | bytes 16777216
  728.3 11.7 %custom-call.60 = f32[128,128]{1,0:T(8,128)S(1)} custom-call(f32[128,128]{1,0:T(8,128)S(1)} %copy.90), custom_call_target="Cholesky" | custom-call | tf_op jit(solution)/shard_map/cholesky/custom-call.1 | solution.py:13
  756.8 11.9 %custom-call.61 = f32[128,128]{1,0:T(8,128)S(1)} custom-call(f32[128,128]{1,0:T(8,128)S(1)} %slice.501), custom_call_target="Cholesky" | custom-call | tf_op jit(solution)/shard_map/cholesky/custom-call.1 | solution.py:13
  (331 shorter events, 356.6 us)
Async XLA Ops:
  7.2 84.9 %all-gather.33.cloned.1.call-start = ((), (), s32[]{:S(2)}) async-start(), calls=%async_computation.13 | async-start | bytes 4718592 | tf_op jit(solution)/shard_map/all_gather | solution.py:54
  15.9 326.9 %all-gather.15.cloned.1.call-start = ((), (), s32[]{:S(2)}) async-start(), calls=%async_computation.4 | async-start | bytes 1769472 | tf_op jit(solution)/shard_map/all_gather | solution.py:67
  125.1 90.4 %copy-start.1 = (f32[128,1280]{1,0:T(8,128)}, f32[128,1280]{1,0:T(8,128)S(1)}, u32[]{:S(2)}) copy-start(f32[128,1280]{1,0:T(8,128)S(1)} %fusion.44) | copy-start | bytes 1966084
  126.0 218.7 %all-gather.17.cloned.1.call-start = ((), (), s32[]{:S(2)}) async-start(), calls=%async_computation.5 | async-start | bytes 1769472 | tf_op jit(solution)/shard_map/all_gather | solution.py:67
  154.9 192.8 %all-gather.19.cloned.1.call-start = ((), (), s32[]{:S(2)}) async-start(), calls=%async_computation.6 | async-start | bytes 1769472 | tf_op jit(solution)/shard_map/all_gather | solution.py:67
  184.8 166.0 %all-gather.21.cloned.1.call-start = ((), (), s32[]{:S(2)}) async-start(), calls=%async_computation.7 | async-start | bytes 1769472 | tf_op jit(solution)/shard_map/all_gather | solution.py:67
  215.3 138.5 %all-gather.23.cloned.1.call-start = ((), (), s32[]{:S(2)}) async-start(), calls=%async_computation.8 | async-start | bytes 1769472 | tf_op jit(solution)/shard_map/all_gather | solution.py:67
  216.7 26.8 %copy-start.2 = (f32[128,1280]{1,0:T(8,128)S(1)}, f32[128,1280]{1,0:T(8,128)}, u32[]{:S(2)}) copy-start(f32[128,1280]{1,0:T(8,128)} %copy-done.1) | copy-start | bytes 1966084
  219.9 24.8 %copy-start.8 = (f32[128,896]{1,0:T(8,128)S(1)}, f32[128,896]{1,0:T(8,128)}, u32[]{:S(2)}) copy-start(f32[128,896]{1,0:T(8,128)} %copy-done.7) | copy-start | bytes 1376260
  246.9 148.6 %all-gather.25.cloned.1.call-start = ((), (), s32[]{:S(2)}) async-start(), calls=%async_computation.9 | async-start | bytes 1769472 | tf_op jit(solution)/shard_map/all_gather | solution.py:67
  277.5 163.1 %all-gather.27.cloned.1.call-start = ((), (), s32[]{:S(2)}) async-start(), calls=%async_computation.10 | async-start | bytes 1769472 | tf_op jit(solution)/shard_map/all_gather | solution.py:67
  313.0 172.8 %all-gather.29.cloned.1.call-start = ((), (), s32[]{:S(2)}) async-start(), calls=%async_computation.11 | async-start | bytes 1769472 | tf_op jit(solution)/shard_map/all_gather | solution.py:67
  513.6 24.5 %all-to-all-start.1 = ((f32[2,4,128,3,128]{2,0,4,3,1:T(2,128)}), f32[2,4,128,3,128]{2,0,4,3,1:T(2,128)}, u32[]{:S(2)}, u32[]{:S(2)}) async-start(f32[2,4,128,3,128]{2,0,4,3,1:T(2,128)} %copy.81), calls=%async_computation.1 | async-start | bytes 3145728 | tf_op jit(solution)/shard_map/all_to_all | solution.py:95
  524.5 5.9 copy-start.11
  538.1 24.5 %all-to-all-start.2 = ((f32[2,4,128,3,128]{2,0,4,3,1:T(2,128)}), f32[2,4,128,3,128]{2,0,4,3,1:T(2,128)}, u32[]{:S(2)}, u32[]{:S(2)}) async-start(f32[2,4,128,3,128]{2,0,4,3,1:T(2,128)} %copy.83), calls=%async_computation.2 | async-start | bytes 3145728 | tf_op jit(solution)/shard_map/all_to_all | solution.py:95
  554.8 11.4 %copy-start.51 = (s32[4,24]{1,0:T(4,128)S(1)}, s32[4,24]{1,0:T(4,128)}, u32[]{:S(2)}) copy-start(s32[4,24]{1,0:T(4,128)} %param.6) | copy-start | bytes 1156
  562.6 23.6 %all-to-all-start = ((f32[2,4,128,3,128]{2,0,4,3,1:T(2,128)}), f32[2,4,128,3,128]{2,0,4,3,1:T(2,128)S(1)}, u32[]{:S(2)}, u32[]{:S(2)}) async-start(f32[2,4,128,3,128]{2,0,4,3,1:T(2,128)} %copy.79), calls=%async_computation | async-start | bytes 3145728 | tf_op jit(solution)/shard_map/all_to_all | solution.py:95
  566.1 145.2 %all-gather.35.cloned.1.call-start = ((), (), s32[]{:S(2)}) async-start(), calls=%async_computation.14 | async-start | bytes 2621440 | tf_op jit(solution)/shard_map/all_gather | solution.py:147
  636.1 6.7 copy-start.6
  638.4 30.1 %all-to-all-start.3 = ((f32[8,256,128]{2,1,0:T(8,128)}), f32[8,256,128]{2,1,0:T(8,128)}, u32[]{:S(2)}, u32[]{:S(2)}) async-start(f32[8,256,128]{2,1,0:T(8,128)} %bitcast.67), calls=%async_computation.3 | async-start | bytes 2097152 | tf_op jit(solution)/shard_map/all_to_all | solution.py:149
  642.7 77.1 %all-gather.31.cloned.1.call-start = ((), (), s32[]{:S(2)}) async-start(), calls=%async_computation.12 | async-start | bytes 2359296 | tf_op jit(solution)/shard_map/all_gather | solution.py:157
  652.8 17.6 %copy-start.48 = (f32[128,128]{1,0:T(8,128)S(1)}, f32[128,128]{1,0:T(8,128)}, u32[]{:S(2)}) copy-start(f32[128,128]{1,0:T(8,128)} %get-tuple-element.12) | copy-start | bytes 196612
  672.3 13.9 %copy-start.14 = (f32[1024,384]{1,0:T(8,128)S(1)}, f32[1024,384]{1,0:T(8,128)}, u32[]{:S(2)}) copy-start(f32[1024,384]{1,0:T(8,128)} %copy-done.13) | copy-start | bytes 4718596
  754.1 30.3 %copy-start.9 = (f32[128,3200]{1,0:T(8,128)}, f32[128,3200]{1,0:T(8,128)S(1)}, u32[]{:S(2)}) copy-start(f32[128,3200]{1,0:T(8,128)S(1)} %fusion.16) | copy-start | bytes 4915204
  (46 other events, 99.4 us)
Sparse Core Ops, SparseCore 0:
  16.0 76.0 all-gather.32
  126.1 42.9 all-gather.14
  171.4 43.1 all-gather.16
  216.6 43.0 all-gather.18
  261.8 42.9 all-gather.20
  306.9 43.0 all-gather.22
  352.2 43.3 all-gather.24
  397.7 42.8 all-gather.26
  442.9 42.8 all-gather.28
  636.2 20.1 all-gather.34
  670.5 49.2 all-gather.30

commit v2 on v1

--- a/solution.py
+++ b/solution.py
@@ -1,6 +1,8 @@
 import jax
 import jax.numpy as jnp
 from jax import lax
+from jax.experimental import pallas as pl
+from jax.experimental.pallas import tpu as pltpu
 from jax.sharding import PartitionSpec as P
 
 CHILD_PIVOTS = 8
@@ -9,12 +11,119 @@
 HIGHEST = lax.Precision.HIGHEST
 
 
-def factor_block(square):
-    return lax.linalg.cholesky(square, symmetrize_input=False)
-
-
-def solve_left(factor, rows):
-    return lax.linalg.triangular_solve(factor, rows, left_side=True, lower=True)
+def strip_kernel(current_ref, strip_ref, square, inverse):
+    n = current_ref.shape[0]
+    width = current_ref.shape[1]
+    square[...] = current_ref[:, :n]
+    rows = lax.broadcasted_iota(jnp.int32, (n, n), 0)
+    lanes = lax.broadcasted_iota(jnp.int32, (n, n), 1)
+    inverse[...] = jnp.where(rows == lanes, 1.0, 0.0)
+    slab_row = lax.broadcasted_iota(jnp.int32, (8, n), 0)
+    slab_lane = lax.broadcasted_iota(jnp.int32, (8, n), 1)
+    for low in range(0, n, 8):
+        top = square[low : low + 8, :]
+        ident = inverse[low : low + 8, :]
+        wide = [
+            jnp.broadcast_to(top[:, low + k : low + k + 1], (8, n)) for k in range(8)
+        ]
+        top = jnp.where(slab_lane >= low, top, 0.0)
+        for k in range(8):
+            pivot = wide[k][k : k + 1, :]
+            root = lax.rsqrt(pivot)
+            root = root * (1.5 - 0.5 * (pivot * root) * root)
+            under = slab_row > k
+            at = slab_row == k
+            scale = jnp.where(under, wide[k] * root, 0.0)
+            keep = jnp.where(at, root, 1.0)
+            for m in range(k + 1, 8):
+                wide[m] = wide[m] - scale * (wide[m][k : k + 1, :] * root)
+            top = top * keep - scale * (top[k : k + 1, :] * root)
+            ident = ident * keep - scale * (ident[k : k + 1, :] * root)
+        top = jnp.where(slab_lane >= low + slab_row, top, 0.0)
+        strip_ref[low : low + 8, :n] = top
+        inverse[low : low + 8, :] = ident
+        if low + 8 < n:
+            both = jnp.concatenate([top, ident], 1)
+            change = lax.dot_general(
+                top, both, (((0,), (0,)), ((), ())),
+                precision=HIGHEST, preferred_element_type=jnp.float32,
+            )
+            square[low + 8 :, :] = square[low + 8 :, :] - change[low + 8 :, :n]
+            inverse[low + 8 :, :] = inverse[low + 8 :, :] - change[low + 8 :, n:]
+    solver = inverse[...]
+    for low in range(n, width, 2 * n):
+        high = min(low + 2 * n, width)
+        strip_ref[:, low:high] = jnp.dot(
+            solver, current_ref[:, low:high],
+            precision=HIGHEST, preferred_element_type=jnp.float32,
+        )
+
+
+def finish_strip(current):
+    block, width = current.shape
+    return pl.pallas_call(
+        strip_kernel,
+        out_shape=jax.ShapeDtypeStruct((block, width), jnp.float32),
+        in_specs=[pl.BlockSpec(memory_space=pltpu.VMEM)],
+        out_specs=pl.BlockSpec(memory_space=pltpu.VMEM),
+        scratch_shapes=[
+            pltpu.VMEM((block, block), jnp.float32),
+            pltpu.VMEM((block, block), jnp.float32),
+        ],
+        compiler_params=pltpu.CompilerParams(vmem_limit_bytes=32 * 1024 * 1024),
+        cost_estimate=pl.CostEstimate(
+            flops=2 * block * block * (width + block),
+            bytes_accessed=8 * block * width,
+            transcendentals=block,
+        ),
+        name="strip",
+    )(current)
+
+
+def extend_kernel(row_ref, col_ref, *refs):
+    parent_ref, out_ref = refs[-2], refs[-1]
+    here = pl.program_id(0)
+    block = parent_ref.shape[0]
+    out_ref[...] = parent_ref[...]
+    for group, child in enumerate(refs[:-2]):
+        for slot in range(child.shape[3] // block):
+            target = col_ref[group, slot]
+
+            @pl.when((row_ref[group, here] >= 0) & (target >= 0))
+            def _():
+                span = pl.ds(pl.multiple_of(target * block, block), block)
+                part = child[0, 0, :, slot * block : (slot + 1) * block]
+                out_ref[:, span] = out_ref[:, span] + part
+
+
+def extend_add(parent, received, row_index, col_index):
+    groups, rslots = row_index.shape
+    block = parent.shape[0] // rslots
+    columns = parent.shape[1]
+    wide = received.shape[3]
+
+    def child_spec(group):
+        return pl.BlockSpec(
+            (1, 1, block, wide),
+            lambda a, rows, cols: (jnp.maximum(rows[group, a], 0), group, 0, 0),
+        )
+
+    return pl.pallas_call(
+        extend_kernel,
+        out_shape=jax.ShapeDtypeStruct(parent.shape, jnp.float32),
+        grid_spec=pltpu.PrefetchScalarGridSpec(
+            num_scalar_prefetch=2,
+            grid=(rslots,),
+            in_specs=[child_spec(group) for group in range(groups)]
+            + [pl.BlockSpec((block, columns), lambda a, rows, cols: (a, 0))],
+            out_specs=pl.BlockSpec((block, columns), lambda a, rows, cols: (a, 0)),
+        ),
+        compiler_params=pltpu.CompilerParams(vmem_limit_bytes=32 * 1024 * 1024),
+        cost_estimate=pl.CostEstimate(
+            flops=parent.size, bytes_accessed=12 * parent.size, transcendentals=0
+        ),
+        name="extend_add",
+    )(row_index, col_index, *([received] * groups), parent)
 
 
 def factor_strips(work, pivots, block):
@@ -29,9 +138,7 @@
             current = current - lax.dot_general(
                 done[:, :block], done, (((0,), (0,)), ((), ())), precision=HIGHEST
             )
-        factor = factor_block(current[:, :block])
-        rest = solve_left(factor, current[:, block:])
-        strips.append(jnp.concatenate([factor.T, rest], 1))
+        strips.append(finish_strip(current))
     return strips
 
 
@@ -51,7 +158,12 @@
     update_count = order // block - pivots
     matrix = child_fronts.reshape(order, slots * block)
 
-    lead = lax.all_gather(matrix[:width, : panel_slots * block], "front", axis=0)
+    lead = matrix[:width, : panel_slots * block]
+    if front_count == pivots:
+        lead = jnp.broadcast_to(lead[None], (front_count,) + lead.shape)
+        lead = lax.all_to_all(lead, "front", split_axis=0, concat_axis=0, tiled=True)
+    else:
+        lead = lax.all_gather(lead, "front", axis=0)
     lead = lead.reshape(front_count, width, panel_slots, block).transpose(1, 2, 0, 3)
     lead = lead.reshape(width, panel_slots * front_count * block)[:, :width]
 
@@ -63,14 +175,17 @@
     for i, strip in enumerate(strips):
         split = width - i * block
         own.append(strip[:, split:])
-        gathered.append(
-            lax.all_gather(strip[:, split:].T, "front", axis=0, tiled=True).reshape(
-                front_count, kept, block, block
-            )
-        )
         column = strip[:, :split].T
         lead_columns.append(
             jnp.concatenate([jnp.zeros((i * block, block), jnp.float32), column], 0)
+        )
+    early = (3 * pivots) // 8
+    for group in (own[:early], own[early:]):
+        sent = jnp.concatenate(group, 0).T
+        gathered.append(
+            lax.all_gather(sent, "front", axis=0, tiled=True).reshape(
+                front_count, kept, block, sent.shape[1]
+            )
         )
     own = jnp.concatenate(own, 0)
     lower = jnp.concatenate(gathered, 3).transpose(1, 0, 2, 3)
@@ -89,7 +204,7 @@
         piece = matrix[width + low : width + low + part_rows, first_slot * block :] - product
         sums.append(piece)
         outgoing = piece.reshape(
-            part_rows // block // leaf_count, leaf_count, block, kept, block
+            part_rows // block // leaf_count, leaf_count, block, kept * block
         )
         received.append(
             lax.all_to_all(outgoing, "leaf", split_axis=1, concat_axis=1, tiled=True)
@@ -129,18 +244,18 @@
     row_map = lax.dynamic_index_in_dim(
         child_map.reshape(groups, quota, leaf_count), leaf_pos, axis=2, keepdims=False
     )
-    row_onehot = (
-        (row_map // leaf_count)[:, :, None] == jnp.arange(rslots)[None, None, :]
-    ).astype(jnp.float32)
+    hits = (row_map // leaf_count)[:, :, None] == jnp.arange(rslots)[None, None, :]
+    steps = jnp.arange(quota, dtype=jnp.int32)[None, :, None]
+    row_index = jnp.max(jnp.where(hits, steps, -1), axis=1)
     col_blocks = jnp.arange(first_slot, slots) * front_count + front_pos - pivots
-    valid = col_blocks >= 0
     col_map = jnp.take(child_map, jnp.clip(col_blocks, 0, update_count - 1), axis=1)
-    col_match = (col_map // front_count)[:, :, None] == jnp.arange(cslots)[None, None, :]
-    col_onehot = (valid[None, :, None] & col_match).astype(jnp.float32)
-    placed = jnp.einsum("gqa,qgxcy->gaxcy", row_onehot, received, precision=HIGH)
-    summed = jnp.einsum("gcb,gaxcy->axby", col_onehot, placed, precision=HIGH)
-    parent = parent_front.reshape(rslots * block, cslots * block)
-    parent = parent + summed.reshape(rslots * block, cslots * block)
+    col_index = jnp.where((col_blocks >= 0)[None, :], col_map // front_count, -1)
+    parent = extend_add(
+        parent_front.reshape(rslots * block, cslots * block),
+        received,
+        row_index.astype(jnp.int32),
+        col_index.astype(jnp.int32),
+    )
 
     count = PARENT_PIVOTS
     span = count * block

time: 820 us -> 641 us (0.78)
  other arithmetic: 257 us -> 20.2 us
  Pallas kernels: 0 us -> 97.8 us
  matrix products: 93.4 us -> 32.3 us
  waiting for transfers between devices: 231 us -> 265 us
  local copies, waits for them, and re-layouts: 186 us -> 168 us
    another operation x42 -> x0, other arithmetic: 225 us -> none  [the longest x30 124 us: factor_block(): return lax.linalg.cholesky(square, symmetrize_input=False)]
    pallas_call x0 -> x11, Pallas kernels: none -> 97.8 us  [the longest x10 94 us: finish_strip(): pl.pallas_call(strip_kernel, out_shape=jax.ShapeDtypeStruct((block, width...]
    all_to_all x0 -> x1, waiting for transfers between devices: none -> 91.7 us  [body(): lax.all_to_all(lead, 'front', split_axis=0, concat_axis=0, tiled=True)]
    all_gather x9 -> x2, waiting for transfers between devices: 186 us -> 130 us  [body(): lax.all_gather(sent, 'front', axis=0, tiled=True)]
    dot_general x2 -> x0, matrix products: 32.4 us -> none  [the longest x1 22.1 us: body(): summed = jnp.einsum('gcb,gaxcy->axby', col_onehot, placed, precision=HIGH)]
    another operation x10 -> x0, matrix products: 16.7 us -> none  [solve_left(): return lax.linalg.triangular_solve(factor, rows, left_side=True, lower=True)]
    reshape x6 -> x4, local copies, waits for them, and re-layouts: 19.3 us -> 5.13 us  [the longest x3 3.77 us: body(): piece.reshape(part_rows // block // leaf_count, leaf_count, block, kept *...]
    add x1 -> x0, other arithmetic: 13.4 us -> none  [body(): parent = parent + summed.reshape(rslots * block, cslots * block)]
  transfers between devices with their start and end apart: 15 -> 9, of which waited for: 9 -> 7; matrix products, arithmetic and copies ran while one was open for 41% -> 19% of each run, Pallas kernels for 0% -> 7%
where the time goes in v2:
time: 641 us; the launch traced here: 630 us
  waiting for transfers between devices  265 us (41%)
  local copies, waits for them, and re-layouts  168 us (26%)
  Pallas kernels  97.8 us (15%)
  matrix products  32.3 us (5%)
  starting transfers between devices  25.1 us (4%)
  other arithmetic  20.2 us (3%)
  between operations  14.9 us (2%)
  blocking collectives  6.92 us (1%)
    all_gather x2, waiting for transfers between devices, body(): lax.all_gather(sent, 'front', axis=0, tiled=True)  130 us
    pallas_call x10, Pallas kernels, finish_strip(): pl.pallas_call(strip_kernel, out_shape=jax.ShapeDtypeStruct((block, width...  94 us
    all_to_all x1, waiting for transfers between devices, body(): lax.all_to_all(lead, 'front', split_axis=0, concat_axis=0, tiled=True)  91.7 us
    unnamed x96, local copies, waits for them, and re-layouts  89.2 us
    all_to_all x3, waiting for transfers between devices, body(): lax.all_to_all(outgoing, 'leaf', split_axis=1, concat_axis=1, tiled=True)  32.3 us
    dot_general x3, matrix products, body(): lax.dot_general(lower[low:low + part_rows], own, (((1,), (0,)), ((), ()))...  18.5 us
    all_gather x2, local copies, waits for them, and re-layouts, body(): lax.all_gather(sent, 'front', axis=0, tiled=True)  15.1 us
    all_to_all x3, starting transfers between devices, body(): lax.all_to_all(outgoing, 'leaf', split_axis=1, concat_axis=1, tiled=True)  13.3 us
  transfers between devices with their start and end apart: 9, of which 7 were waited for; matrix products, arithmetic and copies ran while one was open for 19% of the time, Pallas kernels for 7%

profile of v2, /device:TPU:0, one launch (start us, length us, event | category | flops | bytes accessed | tf_op | source)
XLA Modules:
  0.0 629.7 jit_solution(5448388026323959957)
XLA Ops:
  26.1 91.7 %all-to-all-done = f32[8,1024,128]{2,1,0:T(8,128)} async-done(((f32[8,1024,128]{2,1,0:T(8,128)}), f32[8,1024,128]{2,1,0:T(8,128)}, u32[]{:S(2)}, u32[]{:S(2)}) %all-to-all-start) | async-done | bytes 4194336 | tf_op jit(solution)/shard_map/all_to_all | solution.py:164
  123.5 9.4 %strip.10 = f32[128,1408]{1,0:T(8,128)S(1)} custom-call(f32[128,1408]{1,0:T(8,128)S(1)} %fusion.29.current_ref), custom_call_target="tpu_custom_call" | custom-call | flops 50331648 | bytes 1441792 | tf_op jit(solution)/shard_map/strip/pallas_call | solution.py:64
  134.5 9.7 %strip.11 = f32[128,1280]{1,0:T(8,128)S(1)} custom-call(f32[128,1280]{1,0:T(8,128)S(1)} %convolution_subtract_fusion.2.current_ref), custom_call_target="tpu_custom_call" | custom-call | flops 46137344 | bytes 1310720 | tf_op jit(solution)/shard_map/strip/pallas_call | solution.py:64
  145.1 9.1 %strip.12 = f32[128,1152]{1,0:T(8,128)S(1)} custom-call(f32[128,1152]{1,0:T(8,128)S(1)} %convolution_subtract_fusion.1.current_ref), custom_call_target="tpu_custom_call" | custom-call | flops 41943040 | bytes 1179648 | tf_op jit(solution)/shard_map/strip/pallas_call | solution.py:64
  160.7 9.2 %strip.13 = f32[128,1024]{1,0:T(8,128)S(1)} custom-call(f32[128,1024]{1,0:T(8,128)S(1)} %fusion.15.current_ref), custom_call_target="tpu_custom_call" | custom-call | flops 37748736 | bytes 1048576 | tf_op jit(solution)/shard_map/strip/pallas_call | solution.py:64
  172.0 9.2 %strip.14 = f32[128,896]{1,0:T(8,128)S(1)} custom-call(f32[128,896]{1,0:T(8,128)S(1)} %fusion.18.current_ref), custom_call_target="tpu_custom_call" | custom-call | flops 33554432 | bytes 917504 | tf_op jit(solution)/shard_map/strip/pallas_call | solution.py:64
  183.8 9.1 %strip.15 = f32[128,768]{1,0:T(8,128)S(1)} custom-call(f32[128,768]{1,0:T(8,128)S(1)} %convolution_subtract_fusion.3.current_ref), custom_call_target="tpu_custom_call" | custom-call | flops 29360128 | bytes 786432 | tf_op jit(solution)/shard_map/strip/pallas_call | solution.py:64
  195.1 8.9 %strip.16 = f32[128,640]{1,0:T(8,128)S(1)} custom-call(f32[128,640]{1,0:T(8,128)S(1)} %convolution_subtract_fusion.4.current_ref), custom_call_target="tpu_custom_call" | custom-call | flops 25165824 | bytes 655360 | tf_op jit(solution)/shard_map/strip/pallas_call | solution.py:64
  206.8 9.0 %strip.17 = f32[128,512]{1,0:T(8,128)S(1)} custom-call(f32[128,512]{1,0:T(8,128)S(1)} %convolution_subtract_fusion.5.current_ref), custom_call_target="tpu_custom_call" | custom-call | flops 20971520 | bytes 524288 | tf_op jit(solution)/shard_map/strip/pallas_call | solution.py:64
  220.5 15.8 %all-gather.7.cloned.1.call-done = f32[3072,384]{0,1:T(8,128)} async-done(((f32[384,384]{0,1:T(8,128)}), f32[3072,384]{0,1:T(8,128)}) %all-gather.7.cloned.1.call-update) | async-done | bytes 4718608 | tf_op jit(solution)/shard_map/all_gather | solution.py:186
  242.3 113.8 %all-gather.9.cloned.1.call-done = f32[3072,640]{0,1:T(8,128)} async-done(((f32[384,640]{0,1:T(8,128)}), f32[3072,640]{0,1:T(8,128)}) %all-gather.9.cloned.1.call-update) | async-done | bytes 7864336 | tf_op jit(solution)/shard_map/all_gather | solution.py:186
  356.0 9.1 %copy.75 = f32[3072,640]{1,0:T(8,128)} copy(f32[3072,640]{0,1:T(8,128)} %all-gather.9.cloned.1.call-done) | data formatting | bytes 15728640 | tf_op jit(solution)/shard_map/all_gather | solution.py:186
  365.1 11.6 %maximum_bitcast_fusion = f32[3,8,128,1024]{3,2,0,1:T(8,128)} fusion(f32[8,3,128,640]{3,2,1,0:T(8,128)} %bitcast.115, f32[8,3,128,384]{3,2,1,0:T(8,128)} %bitcast.121), kind=kLoop, calls=%fused_computation.8 | loop fusion | flops 3145728 | bytes 25165824 | tf_op jit(solution)/shard_map/transpose | solution.py:191
  376.7 10.3 %fusion.72 = (f32[1,8,128,1024]{3,2,0,1:T(8,128)}, f32[1,8,128,1024]{3,2,0,1:T(8,128)S(1)}, f32[1,8,128,1024]{3,2,0,1:T(8,128)}) fusion(f32[3,8,128,1024]{3,2,0,1:T(8,128)} %maximum_bitcast_fusion), kind=kLoop, calls=%fused_computation.178 | loop fusion | bytes 25165824 | tf_op jit(solution)/shard_map/slice | solution.py:202
  407.1 11.1 %all-to-all-done.3 = f32[2,4,128,384]{3,2,0,1:T(8,128)} async-done(((f32[2,4,128,384]{3,2,0,1:T(8,128)}), f32[2,4,128,384]{3,2,0,1:T(8,128)}, u32[]{:S(2)}, u32[]{:S(2)}) %all-to-all-start.3) | async-done | bytes 1572896 | tf_op jit(solution)/shard_map/all_to_all | solution.py:210
  431.6 11.2 %all-to-all-done.2 = f32[2,4,128,384]{3,2,0,1:T(8,128)} async-done(((f32[2,4,128,384]{3,2,0,1:T(8,128)}), f32[2,4,128,384]{3,2,0,1:T(8,128)}, u32[]{:S(2)}, u32[]{:S(2)}) %all-to-all-start.2) | async-done | bytes 1572896 | tf_op jit(solution)/shard_map/all_to_all | solution.py:210
  457.2 10.0 %all-to-all-done.1 = f32[2,4,128,384]{3,2,0,1:T(8,128)} async-done(((f32[2,4,128,384]{3,2,0,1:T(8,128)}), f32[2,4,128,384]{3,2,0,1:T(8,128)}, u32[]{:S(2)}, u32[]{:S(2)}) %all-to-all-start.1) | async-done | bytes 1572896 | tf_op jit(solution)/shard_map/all_to_all | solution.py:210
  502.4 10.9 %all-to-all-done.4 = f32[8,256,128]{1,2,0:T(8,128)} async-done(((f32[8,256,128]{1,2,0:T(8,128)}), f32[8,256,128]{1,2,0:T(8,128)}, u32[]{:S(2)}, u32[]{:S(2)}) %all-to-all-start.4) | async-done | bytes 1048608 | tf_op jit(solution)/shard_map/all_to_all | solution.py:264
  516.9 12.1 %copy.76 = f32[3,8,128,1024]{3,2,1,0:T(8,128)} copy(f32[3,8,128,1024]{3,2,0,1:T(8,128)} %maximum_bitcast_fusion) | data formatting | bytes 25165824 | tf_op jit(solution)/shard_map/transpose | solution.py:191
  533.1 22.8 %copy.89 = f32[1,4096,4,1,128]{4,3,2,1,0:T(1,128)} copy(f32[1,4096,4,1,128]{4,1,2,3,0:T(8,128)S(1)} %maximum_bitcast_fusion.1) | data formatting | bytes 16777216
  555.9 9.2 %copy.88 = f32[2048,1024]{0,1:T(8,128)} copy(f32[2048,1024]{1,0:T(8,128)} %copy-done) | data formatting | bytes 16777216 | tf_op jit(solution)/shard_map/extend_add/pallas_call | solution.py:111
  576.3 10.1 %strip.18 = f32[128,3328]{1,0:T(8,128)S(1)} custom-call(f32[128,3328]{1,0:T(8,128)S(1)} %slice.457.current_ref), custom_call_target="tpu_custom_call" | custom-call | flops 113246208 | bytes 3407872 | tf_op jit(solution)/shard_map/strip/pallas_call | solution.py:64
  588.1 10.2 %strip.19 = f32[128,3200]{1,0:T(8,128)S(1)} custom-call(f32[128,3200]{1,0:T(8,128)S(1)} %convolution_subtract_fusion.current_ref), custom_call_target="tpu_custom_call" | custom-call | flops 109051904 | bytes 3276800 | tf_op jit(solution)/shard_map/strip/pallas_call | solution.py:64
  609.9 13.1 %copy.90 = f32[16,1,128,8,1,128]{5,4,3,2,1,0:T(1,128)} copy(f32[16,1,128,8,1,128]{2,0,5,3,4,1:T(8,128)} %bitcast.114) | data formatting | bytes 16777216
  (205 shorter events, 168.3 us)
Async XLA Ops:
  17.3 100.5 %all-to-all-start = ((f32[8,1024,128]{2,1,0:T(8,128)}), f32[8,1024,128]{2,1,0:T(8,128)}, u32[]{:S(2)}, u32[]{:S(2)}) async-start(f32[8,1024,128]{2,1,0:T(8,128)} %broadcast_in_dim.38), calls=%async_computation | async-start | bytes 8388608 | tf_op jit(solution)/shard_map/all_to_all | solution.py:164
  24.5 211.7 %all-gather.7.cloned.1.call-start = ((), (), s32[]{:S(2)}) async-start(), calls=%async_computation.5 | async-start | bytes 5308416 | tf_op jit(solution)/shard_map/all_gather | solution.py:186
  123.5 20.9 %copy-start.9 = (f32[128,8,8,128]{3,1,2,0:T(8,128)}, f32[128,8,8,128]{3,1,2,0:T(8,128)S(1)}, u32[]{:S(2)}) copy-start(f32[128,8,8,128]{3,1,2,0:T(8,128)S(1)} %copy.110) | copy-start | bytes 12582916
  134.5 9.8 %slice-start.3 = ((f32[128,1408]{1,0:T(8,128)}), f32[128,1152]{1,0:T(8,128)S(1)}, s32[]{:S(2)}) async-start(f32[128,1408]{1,0:T(8,128)} %copy-done.1), calls=%async_computation.12 | async-start | bytes 1179648 | tf_op jit(solution)/shard_map/slice | solution.py:136
  144.3 12.7 %copy-start.3 = (f32[128,1280]{1,0:T(8,128)}, f32[128,1280]{1,0:T(8,128)S(1)}, u32[]{:S(2)}) copy-start(f32[128,1280]{1,0:T(8,128)S(1)} %strip.11) | copy-start | bytes 1966084
  156.7 199.4 %all-gather.9.cloned.1.call-start = ((), (), s32[]{:S(2)}) async-start(), calls=%async_computation.6 | async-start | bytes 8847360 | tf_op jit(solution)/shard_map/all_gather | solution.py:186
  160.7 9.3 %copy-start.4 = (f32[128,1280]{1,0:T(8,128)S(1)}, f32[128,1280]{1,0:T(8,128)}, u32[]{:S(2)}) copy-start(f32[128,1280]{1,0:T(8,128)} %copy-done.3) | copy-start | bytes 1966084
  160.7 10.1 %slice-start.4 = ((f32[128,1408]{1,0:T(8,128)}), f32[128,896]{1,0:T(8,128)S(1)}, s32[]{:S(2)}) async-start(f32[128,1408]{1,0:T(8,128)} %copy-done.1), calls=%async_computation.13 | async-start | bytes 917504 | tf_op jit(solution)/shard_map/slice | solution.py:136
  160.7 10.1 %slice-start.7 = ((f32[128,1152]{1,0:T(8,128)}), f32[128,896]{1,0:T(8,128)S(1)}, s32[]{:S(2)}) async-start(f32[128,1152]{1,0:T(8,128)} %copy-done.5), calls=%async_computation.16 | async-start | bytes 917504 | tf_op jit(solution)/shard_map/slice | solution.py:136
  172.0 9.3 %copy-start.6 = (f32[128,1152]{1,0:T(8,128)S(1)}, f32[128,1152]{1,0:T(8,128)}, u32[]{:S(2)}) copy-start(f32[128,1152]{1,0:T(8,128)} %copy-done.5) | copy-start | bytes 1769476
  204.1 283.4 %copy-start.7 = (f32[128,640]{1,0:T(8,128)}, f32[128,640]{1,0:T(8,128)S(1)}, u32[]{:S(2)}) copy-start(f32[128,640]{1,0:T(8,128)S(1)} %strip.16) | copy-start | bytes 983044
  215.8 271.7 %copy-start.8 = (f32[128,512]{1,0:T(8,128)}, f32[128,512]{1,0:T(8,128)S(1)}, u32[]{:S(2)}) copy-start(f32[128,512]{1,0:T(8,128)S(1)} %strip.17) | copy-start | bytes 786436
  393.5 24.7 %all-to-all-start.3 = ((f32[2,4,128,384]{3,2,0,1:T(8,128)}), f32[2,4,128,384]{3,2,0,1:T(8,128)}, u32[]{:S(2)}, u32[]{:S(2)}) async-start(f32[2,4,128,384]{3,2,0,1:T(8,128)} %copy.82), calls=%async_computation.3 | async-start | bytes 3145728 | tf_op jit(solution)/shard_map/all_to_all | solution.py:210
  418.2 24.5 %all-to-all-start.2 = ((f32[2,4,128,384]{3,2,0,1:T(8,128)}), f32[2,4,128,384]{3,2,0,1:T(8,128)}, u32[]{:S(2)}, u32[]{:S(2)}) async-start(f32[2,4,128,384]{3,2,0,1:T(8,128)} %copy.81), calls=%async_computation.2 | async-start | bytes 3145728 | tf_op jit(solution)/shard_map/all_to_all | solution.py:210
  431.5 15.6 %copy-start.23 = (s32[4,24]{1,0:T(4,128)S(1)}, s32[4,24]{1,0:T(4,128)}, u32[]{:S(2)}) copy-start(s32[4,24]{1,0:T(4,128)} %param.5) | copy-start | bytes 1156
  442.7 24.5 %all-to-all-start.1 = ((f32[2,4,128,384]{3,2,0,1:T(8,128)}), f32[2,4,128,384]{3,2,0,1:T(8,128)}, u32[]{:S(2)}, u32[]{:S(2)}) async-start(f32[2,4,128,384]{3,2,0,1:T(8,128)} %copy.80), calls=%async_computation.1 | async-start | bytes 3145728 | tf_op jit(solution)/shard_map/all_to_all | solution.py:210
  447.1 117.9 %all-gather.13.cloned.1.call-start = ((), (), s32[]{:S(2)}) async-start(), calls=%async_computation.8 | async-start | bytes 2621440 | tf_op jit(solution)/shard_map/all_gather | solution.py:262
  483.2 30.1 %all-to-all-start.4 = ((f32[8,256,128]{1,2,0:T(8,128)}), f32[8,256,128]{1,2,0:T(8,128)}, u32[]{:S(2)}, u32[]{:S(2)}) async-start(f32[8,256,128]{1,2,0:T(8,128)} %copy.86), calls=%async_computation.4 | async-start | bytes 2097152 | tf_op jit(solution)/shard_map/all_to_all | solution.py:264
  487.4 78.9 %all-gather.11.cloned.1.call-start = ((), (), s32[]{:S(2)}) async-start(), calls=%async_computation.7 | async-start | bytes 2359296 | tf_op jit(solution)/shard_map/all_gather | solution.py:272
  487.5 8.2 %slice-start.8 = ((f32[128,640]{1,0:T(8,128)}), f32[128,256]{1,0:T(8,128)S(1)}, s32[]{:S(2)}) async-start(f32[128,640]{1,0:T(8,128)} %copy-done.7), calls=%async_computation.17 | async-start | bytes 262144 | tf_op jit(solution)/shard_map/slice | solution.py:178
  488.8 7.6 %slice-start.9 = ((f32[128,512]{1,0:T(8,128)}), f32[128,128]{1,0:T(8,128)S(1)}, s32[]{:S(2)}) async-start(f32[128,512]{1,0:T(8,128)} %copy-done.8), calls=%async_computation.18 | async-start | bytes 131072 | tf_op jit(solution)/shard_map/slice | solution.py:178
  576.3 10.1 %copy-start.16 = (f32[2048,256]{0,1:T(8,128)S(1)}, f32[2048,256]{0,1:T(8,128)}, u32[]{:S(2)}) copy-start(f32[2048,256]{0,1:T(8,128)} %all-gather.11.cloned.1.call-done) | copy-start | bytes 6291460
  586.4 12.1 %slice-start.10 = ((s8[8388608]{0:T(1024)(128)(4,1)}), s8[4194304]{0:T(1024)(128)(4,1)S(1)}, s32[]{:S(2)}) async-start(s8[8388608]{0:T(1024)(128)(4,1)} %bitcast.112), calls=%async_computation.19 | async-start | bytes 8388608
  588.0 10.6 %slice-start.11 = ((s8[8388608]{0:T(1024)(128)(4,1)}), s8[4194304]{0:T(1024)(128)(4,1)S(1)}, s32[]{:S(2)}) async-start(s8[8388608]{0:T(1024)(128)(4,1)} %bitcast.112), calls=%async_computation.20 | async-start | bytes 8388608
  (21 other events, 53.4 us)
Sparse Core Ops, SparseCore 0:
  156.8 79.3 all-gather.6
  238.9 117.0 all-gather.8
  480.7 19.8 all-gather.12
  515.1 49.2 all-gather.10
